TPU v7x, 32 devices: a whole 2x2x4 slice. The times are simulated.
32 devices in a mesh: seg: 8 (over y, x, core), row: 4 (over z).
Axes of the slice: x: 2, y: 2, z: 4, core: 2. Of those that a mesh axis runs over, the one named last changes fastest.
Arguments:
- left_env: bfloat16 [8, 512, 12, 512], P('seg', 'row'), may hold values from -4 to 4, as said below
- right_env: bfloat16 [8, 512, 12, 512], P('seg'), may hold values from -4 to 4, as said below
- site_operator: bfloat16 [4, 12, 12, 4], replicated, may hold values from -1 to 2, as said below
- start_vector: float32 [8, 512, 4, 512], P('seg', 'row'), may hold values from -6 to 6
Outputs:
- last_vector: float32 [8, 512, 4, 512], P('seg', 'row')
- alpha_values: float32 [8, 2], P('seg')
- beta_values: float32 [8, 2], P('seg')
Inputs may be any that keep to these rules, and one draw needn't show every extreme that they name: left_env[i, a, w, c] = left_env[i, c, w, a]. right_env[i, a, w, c] = right_env[i, c, w, a]. site_operator[s, v, w, r] = site_operator[r, v, w, s].
All inputs are finite; a program needn't handle non-finite values.
Results may differ from a plain program's by a relative error of at most 0.0076.
Values may be sent and summed in bfloat16 or wider, within the bound.
A program may use at most 128 MiB of HBM per device.

v0:
```python
import jax
import jax.numpy as jnp
from jax import lax
from jax.sharding import PartitionSpec as P

ITERS = 2


def passed_along(value, axis, steps):
    count = lax.axis_size(axis)
    initial, last = (max(0, -steps), min(count, count - steps))
    return lax.ppermute(value, axis, [(source, source + steps) for source in range(initial, last)])


def local(left_env, right_env, site_operator, start_vector):
    rows_here = left_env.shape[1]
    channels = left_env.shape[2]
    bond_width = left_env.shape[3]
    physical = site_operator.shape[0]
    entries = float(bond_width * physical * bond_width)
    left_local = left_env[0]
    operator_mat = site_operator.reshape(physical * channels, channels * physical)
    last_segment = lax.axis_index("seg") == lax.axis_size("seg") - 1
    received = passed_along(right_env, "seg", -1)
    right_used = jnp.where(last_segment, right_env, received)
    right_mat = right_used[0].reshape(bond_width, channels * bond_width)
    start_local = start_vector[0]
    norm_start = lax.psum(jnp.sum(start_local * start_local), "row") / entries
    current = start_local / jnp.sqrt(norm_start + 1e-06)
    previous = jnp.zeros_like(current)
    beta_prev = jnp.zeros((), jnp.float32)
    alpha_list = []
    beta_list = []
    for step_index in range(ITERS):
        lowered = current.astype(jnp.bfloat16)
        gathered = lax.all_gather(lowered, "row", axis=0, tiled=True)
        contracted = jnp.dot(
            left_local.reshape(rows_here * channels, bond_width),
            gathered.reshape(bond_width, physical * bond_width),
            preferred_element_type=jnp.float32,
        )
        contracted = contracted.astype(jnp.bfloat16).reshape(
            rows_here, channels * physical, bond_width
        )
        mixed = jnp.einsum(
            "ik,akb->aib", operator_mat, contracted, preferred_element_type=jnp.float32
        )
        mixed = mixed.astype(jnp.bfloat16).reshape(rows_here, physical, channels * bond_width)
        image = jnp.einsum("asc,bc->asb", mixed, right_mat, preferred_element_type=jnp.float32)
        image_image, image_curr, image_prev, curr_curr, prev_prev, curr_prev = lax.psum(
            (
                jnp.sum(image * image),
                jnp.sum(image * current),
                jnp.sum(image * previous),
                jnp.sum(current * current),
                jnp.sum(previous * previous),
                jnp.sum(current * previous),
            ),
            "row",
        )
        alpha = image_curr / entries
        norm_sq = (
            image_image
            - 2.0 * alpha * image_curr
            - 2.0 * beta_prev * image_prev
            + alpha * alpha * curr_curr
            + beta_prev * beta_prev * prev_prev
            + 2.0 * alpha * beta_prev * curr_prev
        ) / entries
        residual_vec = image - alpha * current - beta_prev * previous
        beta_next = jnp.sqrt(norm_sq + 1e-06)
        previous = current
        current = residual_vec / beta_next
        beta_prev = beta_next
        alpha_list.append(alpha)
        beta_list.append(beta_next)
    alpha_values = jnp.stack(alpha_list).reshape(1, ITERS)
    beta_values = jnp.stack(beta_list).reshape(1, ITERS)
    return (current[None], alpha_values, beta_values)


def solution(mesh):
    placed = (
        P("seg", "row", None, None),
        P("seg", None, None, None),
        P(),
        P("seg", "row", None, None),
    )
    return jax.shard_map(
        local,
        mesh=mesh,
        in_specs=placed,
        out_specs=(P("seg", "row", None, None), P("seg", None), P("seg", None)),
        check_vma=False,
    )
```

profile of v0, /device:TPU:4, one launch (start us, length us, event | category | flops | bytes accessed | tf_op | source)
XLA Modules:
  0.0 299.3 jit_solution(16806568525329012419)
XLA Ops:
  7.2 8.7 %copy.18 = bf16[1,512,12,512]{1,3,2,0:T(8,128)(2,1)} copy(bf16[1,512,12,512]{3,1,2,0:T(8,128)(2,1)} %param.5) | data formatting | bytes 12582912 | tf_op args[1]
  15.9 2.9 collective-permute-start
  18.9 1.1 multiply_reduce_fusion.5
  20.0 12.6 %psum.87 = f32[]{:T(128)} all-reduce(f32[]{:T(128)} %multiply_reduce_fusion.5), channel_id=1, replica_groups=mesh['seg'=8,'row'=4] {'row'}, use_global_device_ids=true, to_apply=%region_1.2 | all-reduce | flops 1 | bytes 8 | tf_op jit(solution)/shard_map/psum | solution.py:28
  33.3 1.1 bitcast_convert_fusion
  34.4 2.3 copy.13
  36.7 1.4 reshape_squeeze.7
  38.1 0.2 copy.15
  38.3 0.1 reshape.38
  38.4 40.1 %all-gather.3.cloned.1.call-done = bf16[512,4,512]{2,0,1:T(8,128)(2,1)} async-done(((bf16[128,4,512]{2,0,1:T(8,128)(2,1)}), bf16[512,4,512]{2,0,1:T(8,128)(2,1)}) %all-gather.3.cloned.1.call-update) | async-done | bytes 2097168 | tf_op jit(solution)/shard_map/all_gather | solution.py:36
  78.5 2.8 copy.12
  81.3 6.7 %fusion = bf16[1536,2048]{0,1:T(8,128)(2,1)} fusion(bf16[512,2048]{0,1:T(8,128)(2,1)S(1)} %bitcast.73, bf16[1536,512]{1,0:T(8,128)(2,1)} %reshape_squeeze.7), kind=kOutput, calls=%fused_computation.2 | convolution fusion | flops 3224371200 | bytes 9961472 | tf_op jit(solution)/shard_map/dot_general | solution.py:37
  88.1 8.6 %copy.14 = bf16[1536,2048]{1,0:T(8,128)(2,1)} copy(bf16[1536,2048]{0,1:T(8,128)(2,1)} %fusion) | data formatting | bytes 12582912 | tf_op jit(solution)/shard_map/convert_element_type | solution.py:42
  96.7 10.7 %reshape.37 = bf16[128,48,512]{2,1,0:T(8,128)(2,1)} reshape(bf16[1536,2048]{1,0:T(8,128)(2,1)} %copy.14) | data formatting | bytes 12582912 | tf_op jit(solution)/shard_map/reshape | solution.py:42
  107.4 7.3 %convert_bitcast_fusion.1 = bf16[128,48,512]{2,1,0:T(8,128)(2,1)} fusion(bf16[128,48,512]{2,1,0:T(8,128)(2,1)} %reshape.37, bf16[48,48]{0,1:T(8,128)(2,1)S(1)} %reshape.38), kind=kOutput, calls=%fused_computation.9 | convolution fusion | flops 305135616 | bytes 12587520 | tf_op jit(solution)/shard_map/ik,akb->aib/dot_general | solution.py:45
  114.7 13.6 %reshape.39 = bf16[128,4,6144]{2,1,0:T(4,128)(2,1)} reshape(bf16[128,48,512]{2,1,0:T(8,128)(2,1)} %convert_bitcast_fusion.1) | data formatting | bytes 12582912 | tf_op jit(solution)/shard_map/reshape | solution.py:48
  128.3 6.1 %broadcast_select_fusion = bf16[1,512,12,512]{1,3,2,0:T(8,128)(2,1)} fusion(bf16[1,512,12,512]{1,3,2,0:T(8,128)(2,1)} %copy.18, bf16[1,512,12,512]{1,3,2,0:T(8,128)(2,1)} %collective-permute-done, pred[]{:T(512)S(6)} %eq.3), kind=kLoop, calls=%fused_computation.10 | loop fusion | flops 3145728 | bytes 18874368 | tf_op jit(solution)/shard_map/jit(_where)/select_n | solution.py:25
  134.4 11.5 %fusion.10 = (f32[]{:T(128)}, f32[]{:T(128)}, f32[]{:T(128)}, f32[]{:T(128)}, f32[]{:T(128)}, /*index=5*/f32[128,4,512]{2,0,1:T(8,128)S(1)}) fusion(f32[]{:T(128)S(6)} %sqrt.9, f32[1,128,4,512]{3,2,1,0:T(4,128)S(1)} %copy-done, bf16[512,6144,1]{0,1,2:T(8,128)(2,1)} %bitcast.70, bf16[128,4,6144]{2,1,0:T(4,128)(2,1)} %reshape.39), kind=kOutput, calls=%fused_computation.23 | convolution fusion | flops 3224109056 | bytes 14680088 | tf_op jit(solution)/shard_map/asc,bc->asb/dot_general | solution.py:49
  145.9 10.9 %all-reduce.1 = (f32[]{:T(128)}, f32[]{:T(128)}, f32[]{:T(128)}, f32[]{:T(128)}, f32[]{:T(128)}, /*index=5*/f32[]{:T(128)}) all-reduce(f32[]{:T(128)} %get-tuple-element.18, f32[]{:T(128)} %get-tuple-element.16, f32[]{:T(128)} %get-tuple-element.17, f32[]{:T(128)} %get-tuple-element.15, ...), channel_id=1, replica_groups=mesh['seg'=8,'row'=4] {'row'}, use_global_device_ids=true, to_apply=%region_5.6 | all-reduce | flops 6 | bytes 48 | tf_op jit(solution)/shard_map/psum | solution.py:50
  163.9 1.2 fusion.18
  165.8 43.9 %all-gather.5.cloned.1.call-done = bf16[512,4,512]{2,0,1:T(8,128)(2,1)} async-done(((bf16[128,4,512]{2,0,1:T(8,128)(2,1)}), bf16[512,4,512]{2,0,1:T(8,128)(2,1)}) %all-gather.5.cloned.1.call-update) | async-done | bytes 2097168 | tf_op jit(solution)/shard_map/all_gather | solution.py:36
  209.7 4.2 %copy.21 = bf16[512,4,512]{0,2,1:T(8,128)(2,1)} copy(bf16[512,4,512]{2,0,1:T(8,128)(2,1)} %all-gather.5.cloned.1.call-done) | data formatting | bytes 4194304 | tf_op jit(solution)/shard_map/all_gather | solution.py:36
  213.8 8.2 %fusion.1 = bf16[1536,2048]{0,1:T(8,128)(2,1)} fusion(bf16[512,2048]{0,1:T(8,128)(2,1)} %bitcast.72, bf16[1536,512]{1,0:T(8,128)(2,1)} %reshape_squeeze.7), kind=kOutput, calls=%fused_computation.3 | convolution fusion | flops 3224371200 | bytes 9961472 | tf_op jit(solution)/shard_map/dot_general | solution.py:37
  222.0 8.6 %copy.22 = bf16[1536,2048]{1,0:T(8,128)(2,1)} copy(bf16[1536,2048]{0,1:T(8,128)(2,1)} %fusion.1) | data formatting | bytes 12582912 | tf_op jit(solution)/shard_map/convert_element_type | solution.py:42
  230.6 10.7 %reshape.41 = bf16[128,48,512]{2,1,0:T(8,128)(2,1)} reshape(bf16[1536,2048]{1,0:T(8,128)(2,1)} %copy.22) | data formatting | bytes 12582912 | tf_op jit(solution)/shard_map/reshape | solution.py:42
  241.3 7.2 %convert_bitcast_fusion = bf16[128,48,512]{2,1,0:T(8,128)(2,1)} fusion(bf16[128,48,512]{2,1,0:T(8,128)(2,1)} %reshape.41, bf16[48,48]{0,1:T(8,128)(2,1)S(1)} %reshape.38), kind=kOutput, calls=%fused_computation.8 | convolution fusion | flops 305135616 | bytes 12587520 | tf_op jit(solution)/shard_map/ik,akb->aib/dot_general | solution.py:45
  248.6 13.6 %reshape.42 = bf16[128,4,6144]{2,1,0:T(4,128)(2,1)} reshape(bf16[128,48,512]{2,1,0:T(8,128)(2,1)} %convert_bitcast_fusion) | data formatting | bytes 12582912 | tf_op jit(solution)/shard_map/reshape | solution.py:48
  262.1 11.5 %fusion.15 = (f32[]{:T(128)}, f32[]{:T(128)}, f32[]{:T(128)}, f32[]{:T(128)}, f32[]{:T(128)}, /*index=5*/f32[128,4,512]{2,0,1:T(8,128)S(1)}) fusion(f32[128,4,512]{2,0,1:T(8,128)S(1)} %get-tuple-element.31, f32[]{:T(128)S(6)} %sqrt.9, f32[1,128,4,512]{3,2,1,0:T(4,128)S(1)} %copy-done, bf16[512,6144,1]{0,1,2:T(8,128)(2,1)} %bitcast.71, ...), kind=kOutput, calls=%fused_computation.28 | convolution fusion | flops 3224109056 | bytes 15728664 | tf_op jit(solution)/shard_map/asc,bc->asb/dot_general | solution.py:49
  273.6 10.2 %all-reduce = (f32[]{:T(128)}, f32[]{:T(128)}, f32[]{:T(128)}, f32[]{:T(128)}, f32[]{:T(128)}) all-reduce(f32[]{:T(128)} %get-tuple-element.12, f32[]{:T(128)} %get-tuple-element.11, f32[]{:T(128)} %get-tuple-element.10, f32[]{:T(128)} %get-tuple-element.13, f32[]{:T(128)} %get-tuple-element.9), channel_id=1, replica_groups=mesh['seg'=8,'row'=4] {'row'}, use_global_device_ids=true, to_apply=%region_16.17 | all-reduce | flops 5 | bytes 40 | tf_op jit(solution)/shard_map/psum | solution.py:50
  289.7 0.5 fusion.13
  290.2 1.6 copy.26
  291.8 0.6 maximum_bitcast_fusion
  (9 shorter events, 0.1 us)
Async XLA Ops:
  7.2 11.7 %copy-start = (f32[1,128,4,512]{3,2,1,0:T(4,128)S(1)}, f32[1,128,4,512]{3,2,1,0:T(4,128)}, u32[]{:S(2)}) copy-start(f32[1,128,4,512]{3,2,1,0:T(4,128)} %param.7) | copy-start | bytes 3145732
  7.2 71.4 %all-gather.3.cloned.1.call-start = ((), (), s32[]{:S(2)}) async-start(), calls=%async_computation | async-start | bytes 2621440 | tf_op jit(solution)/shard_map/all_gather | solution.py:36
  15.9 22.2 %copy-start.1 = (bf16[4,12,12,4]{2,3,1,0:T(4,128)(2,1)S(1)}, bf16[4,12,12,4]{2,3,1,0:T(4,128)(2,1)}, u32[]{:S(2)}) copy-start(bf16[4,12,12,4]{2,3,1,0:T(4,128)(2,1)} %param.6) | copy-start | bytes 13828
  15.9 112.4 %collective-permute-start = (bf16[1,512,12,512]{1,3,2,0:T(8,128)(2,1)}, bf16[1,512,12,512]{1,3,2,0:T(8,128)(2,1)}, u32[]{:S(2)}, u32[]{:S(2)}) collective-permute-start(bf16[1,512,12,512]{1,3,2,0:T(8,128)(2,1)} %copy.18), channel_id=1, source_target_pairs={{4,0},{8,4},{12,8},{16,12},{20,16},{24,20},{28,24},{5,1},{9,5},{13... | collective-permute-start | bytes 18874376 | tf_op jit(solution)/shard_map/ppermute | solution.py:12
  34.4 175.3 %all-gather.5.cloned.1.call-start = ((), (), s32[]{:S(2)}) async-start(), calls=%async_computation.1 | async-start | bytes 2621440 | tf_op jit(solution)/shard_map/all_gather | solution.py:36
Sparse Core Ops, SparseCore 0:
  34.5 44.0 all-gather.2
  165.2 44.3 all-gather.4
where the time goes:
time: 303 us; the launch traced here: 299 us
  local copies, waits for them, and re-layouts  87.1 us (29%)
  waiting for transfers between devices  84 us (28%)
  matrix products  52.4 us (17%)
  blocking collectives  33.7 us (11%)
  between operations  28.4 us (9%)
  other arithmetic  10.6 us (3%)
    all_gather x2, waiting for transfers between devices, local(): gathered = lax.all_gather(lowered, 'row', axis=0, tiled=True)  84 us
    reshape x2, local copies, waits for them, and re-layouts, local(): mixed.astype(jnp.bfloat16)  27.2 us
    dot_general x2, matrix products, local(): jnp.einsum('asc,bc->asb', mixed, right_mat, preferred_element_type=jnp.fl...  22.9 us
    reshape x2, local copies, waits for them, and re-layouts, local(): contracted.astype(jnp.bfloat16)  21.4 us
    psum x2, blocking collectives, local(): lax.psum((jnp.sum(image * image), jnp.sum(image * current), jnp.sum(image...  21.1 us
    convert_element_type x2, local copies, waits for them, and re-layouts, local(): contracted.astype(jnp.bfloat16)  17.2 us
    dot_general x2, matrix products, local(): jnp.dot(left_local.reshape(rows_here * channels, bond_width), gathered.re...  14.9 us
    dot_general x2, matrix products, local(): jnp.einsum('ik,akb->aib', operator_mat, contracted, preferred_element_typ...  14.6 us
  transfers between devices with their start and end apart: 3, of which 2 were waited for; matrix products, arithmetic and copies ran while one was open for 19% of the time, Pallas kernels for 0%

commit v1 on v0

v1 whole, which is shorter than its diff:
```python
import functools

import jax
import jax.numpy as jnp
from jax import lax
from jax.experimental import pallas as pl
from jax.experimental.pallas import tpu as pltpu
from jax.sharding import PartitionSpec as P

ITERS = 2
GROUP = 16
CHUNKS = 4
MESH = pl.DeviceIdType.MESH


def kernel(
    n, segs, dp, width,
    l_ref, r_hbm, o_ref, x_ref,
    out_ref, scalar_ref,
    xg, t_ref, z_ref, r_ref, y_ref, q_ref, red,
    gsend, grecv, ssend, srecv, rsend, rrecv, rlocal,
):
    here, bond = l_ref.shape[1], l_ref.shape[2]
    entries = float(bond * dp * bond)
    seg, me = lax.axis_index("seg"), lax.axis_index("row")
    last = seg == segs - 1

    barrier = pltpu.get_barrier_semaphore()
    for k in range(1, n):
        pl.semaphore_signal(
            barrier, inc=1, device_id={"row": lax.rem(me + k, n)}, device_id_type=MESH
        )

    for k in (1, segs - 1):
        pl.semaphore_signal(
            barrier, inc=1, device_id={"seg": lax.rem(seg + k, segs)}, device_id_type=MESH
        )

    xg[0, :, pl.ds(me * here, here), :] = x_ref[...].astype(jnp.bfloat16).reshape(dp, here, bond)
    pl.semaphore_wait(barrier, n + 1)

    depth = width * bond // CHUNKS

    def right_copy(c):
        rows = pl.ds(c * depth, depth)
        return pltpu.make_async_remote_copy(
            src_ref=r_hbm.at[rows], dst_ref=r_ref.at[rows],
            send_sem=rsend.at[c], recv_sem=rrecv.at[c],
            device_id={"seg": seg - 1}, device_id_type=MESH,
        )

    def right_local(c):
        rows = pl.ds(c * depth, depth)
        return pltpu.make_async_copy(r_hbm.at[rows], r_ref.at[rows], rlocal.at[c])

    def vector_copy(it, way, step, block):
        rows = pl.ds(block * here, here)
        return pltpu.make_async_remote_copy(
            src_ref=xg.at[it, :, rows, :], dst_ref=xg.at[it, :, rows, :],
            send_sem=gsend.at[it, way, step], recv_sem=grecv.at[it, way, step],
            device_id={"row": me + (1 if way == 0 else -1)}, device_id_type=MESH,
        )

    def send_up(step):
        return jnp.logical_and(me < n - 1, me >= step)

    def send_down(step):
        return jnp.logical_and(me > 0, me + step <= n - 1)

    def gather_start(it, step):
        @pl.when(send_up(step))
        def _():
            vector_copy(it, 0, step, me - step).start()

        @pl.when(send_down(step))
        def _():
            vector_copy(it, 1, step, me + step).start()

    def gather_finish(it, step):
        @pl.when(me >= step + 1)
        def _():
            vector_copy(it, 0, step, me - 1 - step).wait_recv()

        @pl.when(me + 1 + step <= n - 1)
        def _():
            vector_copy(it, 1, step, me + 1 + step).wait_recv()

    def total(parts, it):
        row = lax.broadcasted_iota(jnp.int32, (8, 128), 0)
        tile = jnp.zeros((8, 128), jnp.float32)
        for i, part in enumerate(parts):
            tile = jnp.where(row == i, jnp.sum(part, keepdims=True), tile)
        red[it, me] = tile
        copies = []
        for k in range(1, n):
            copies.append(pltpu.make_async_remote_copy(
                src_ref=red.at[it, me], dst_ref=red.at[it, me],
                send_sem=ssend.at[it, k], recv_sem=srecv.at[it, k],
                device_id={"row": lax.rem(me + k, n)}, device_id_type=MESH,
            ))
        for copy in copies:
            copy.start()
        for k in range(1, n):
            other = lax.rem(me + n - k, n)
            pltpu.make_async_remote_copy(
                src_ref=red.at[it, other], dst_ref=red.at[it, other],
                send_sem=ssend.at[it, k], recv_sem=srecv.at[it, k],
                device_id={"row": other}, device_id_type=MESH,
            ).wait_recv()
        whole = red[it, 0]
        for j in range(1, n):
            whole = whole + red[it, j]
        for copy in copies:
            copy.wait_send()
        return [whole[i:i + 1, 0:1] for i in range(len(parts))]

    def apply(it):
        for step in range(n - 1):
            if step:
                gather_start(it, step)
            gather_finish(it, step)

        @pl.loop(0, dp * (width // 4))
        def _(i):
            r, m = i // (width // 4), i % (width // 4)
            rows = l_ref[pl.ds(m * 4, 4)].reshape(4 * here, bond)
            part = jnp.dot(rows, xg[it, r], preferred_element_type=jnp.float32)
            t_ref[r, pl.ds(m * 4, 4)] = part.astype(jnp.bfloat16).reshape(4, here, bond)

        @pl.loop(0, here // GROUP)
        def _(g):
            rows = pl.ds(pl.multiple_of(g * GROUP, GROUP), GROUP)
            t = t_ref[:, :, rows, :].reshape(dp * width * GROUP, bond)
            z = jnp.dot(o_ref[...], t, preferred_element_type=jnp.float32)
            z = z.astype(jnp.bfloat16).reshape(width, dp, GROUP, bond)
            for v in range(width):
                z_ref[:, rows, v * bond:(v + 1) * bond] = z[v]

        for c in range(CHUNKS):
            if it == 0:
                @pl.when(last)
                def _():
                    right_local(c).wait()

                @pl.when(jnp.logical_not(last))
                def _():
                    right_copy(c).wait_recv()

            z = z_ref[:, :, c * depth:(c + 1) * depth].reshape(dp * here, depth)
            part = jnp.dot(z, r_ref[c * depth:(c + 1) * depth, :], preferred_element_type=jnp.float32)
            if c == 0:
                y_ref[...] = part
            else:
                y_ref[...] += part

    gather_start(0, 0)
    for c in range(CHUNKS):
        @pl.when(seg > 0)
        def _():
            right_copy(c).start()

        @pl.when(last)
        def _():
            right_local(c).start()

    apply(0)
    x, y = x_ref[...], y_ref[...]
    xx, xy, yy = total([x * x, x * y, y * y], 0)
    inv = 1.0 / jnp.sqrt(xx / entries + 1e-06)
    xx, xy, yy = xx * inv * inv, xy * inv * inv, yy * inv * inv
    alpha0 = xy / entries
    beta0 = jnp.sqrt((yy - 2.0 * alpha0 * xy + alpha0 * alpha0 * xx) / entries + 1e-06)
    q = (y_ref[...] * inv - (alpha0 * inv) * x_ref[...]) * (1.0 / beta0)
    q_ref[...] = q
    xg[1, :, pl.ds(me * here, here), :] = q.astype(jnp.bfloat16).reshape(dp, here, bond)
    gather_start(1, 0)
    apply(1)
    x, y, q = x_ref[...] * inv, y_ref[...], q_ref[...]
    yy, yq, yx, qq, qx = total([y * y, y * q, y * x, q * q, q * x], 1)
    alpha1 = yq / entries
    norm = (
        yy - 2.0 * alpha1 * yq - 2.0 * beta0 * yx + alpha1 * alpha1 * qq
        + beta0 * beta0 * xx + 2.0 * alpha1 * beta0 * qx
    ) / entries
    beta1 = jnp.sqrt(norm + 1e-06)
    out_ref[...] = (
        y_ref[...] - alpha1 * q_ref[...] - (beta0 * inv) * x_ref[...]
    ) * (1.0 / beta1)
    row = lax.broadcasted_iota(jnp.int32, (8, 128), 0)
    tile = jnp.zeros((8, 128), jnp.float32)
    for i, value in enumerate((alpha0, alpha1, beta0, beta1)):
        tile = jnp.where(row == i, value, tile)
    scalar_ref[...] = tile

    for it in range(ITERS):
        for step in range(n - 1):
            @pl.when(send_up(step))
            def _():
                vector_copy(it, 0, step, me - step).wait_send()

            @pl.when(send_down(step))
            def _():
                vector_copy(it, 1, step, me + step).wait_send()
    for c in range(CHUNKS):
        @pl.when(seg > 0)
        def _():
            right_copy(c).wait_send()


def local(n, segs, left_env, right_env, site_operator, start_vector):
    _, here, width, bond = left_env.shape
    dp = site_operator.shape[0]
    left = jnp.transpose(left_env[0], (1, 0, 2))
    right = jnp.transpose(right_env[0], (1, 0, 2)).reshape(width * bond, bond)
    start = jnp.transpose(start_vector[0], (1, 0, 2)).reshape(dp * here, bond)
    mix = jnp.transpose(site_operator, (1, 0, 3, 2)).reshape(width * dp, dp * width)
    size = width * dp * GROUP
    wide = jnp.repeat(jnp.repeat(mix, GROUP, axis=0), GROUP, axis=1)
    row = lax.broadcasted_iota(jnp.int32, (size, size), 0) % GROUP
    col = lax.broadcasted_iota(jnp.int32, (size, size), 1) % GROUP
    wide = jnp.where(row == col, wide, jnp.zeros_like(wide))
    vmem = pl.BlockSpec(memory_space=pltpu.VMEM)
    dma = pltpu.SemaphoreType.DMA
    steps = max(n - 1, 1)
    result, scalars = pl.pallas_call(
        functools.partial(kernel, n, segs, dp, width),
        out_shape=(
            jax.ShapeDtypeStruct((dp * here, bond), jnp.float32),
            jax.ShapeDtypeStruct((8, 128), jnp.float32),
        ),
        in_specs=[vmem, pl.BlockSpec(memory_space=pl.ANY), vmem, vmem],
        out_specs=(vmem, vmem),
        scratch_shapes=[
            pltpu.VMEM((ITERS, dp, n * here, bond), jnp.bfloat16),
            pltpu.VMEM((dp, width, here, bond), jnp.bfloat16),
            pltpu.VMEM((dp, here, width * bond), jnp.bfloat16),
            pltpu.VMEM((width * bond, bond), jnp.bfloat16),
            pltpu.VMEM((dp * here, bond), jnp.float32),
            pltpu.VMEM((dp * here, bond), jnp.float32),
            pltpu.VMEM((ITERS, n, 8, 128), jnp.float32),
            dma((ITERS, 2, steps)), dma((ITERS, 2, steps)),
            dma((ITERS, n)), dma((ITERS, n)),
            dma((CHUNKS,)), dma((CHUNKS,)), dma((CHUNKS,)),
        ],
        compiler_params=pltpu.CompilerParams(
            collective_id=0, has_side_effects=True, vmem_limit_bytes=50 * 2**20
        ),
    )(left, right, wide, start)
    last = jnp.transpose(result.reshape(dp, here, bond), (1, 0, 2))[None]
    return last, scalars[0:2, 0].reshape(1, 2), scalars[2:4, 0].reshape(1, 2)


def solution(mesh):
    return jax.shard_map(
        functools.partial(local, mesh.shape["row"], mesh.shape["seg"]),
        mesh=mesh,
        in_specs=(
            P("seg", "row", None, None),
            P("seg", None, None, None),
            P(),
            P("seg", "row", None, None),
        ),
        out_specs=(P("seg", "row", None, None), P("seg", None), P("seg", None)),
        check_vma=False,
    )
```

time: 303 us -> 129 us (0.43)
  the two profiles are of different devices: /device:TPU:4 before, /device:TPU:5 now
where the time goes in v1:
time: 129 us
  Pallas kernels  123 us (95%)
  local copies, waits for them, and re-layouts  4.45 us (3%)
    pallas_call x1, Pallas kernels, local(): pl.pallas_call(functools.partial(kernel, n, segs, dp, width), out_shape=(...  123 us

profile of v1, /device:TPU:5, one launch (start us, length us, event | category | flops | bytes accessed | tf_op | source)
XLA Modules:
  0.0 128.6 jit_solution(5117193394658718026)
XLA Ops:
  0.6 0.8 copy.14
  1.5 0.1 reshape.25
  1.6 0.1 copy.15
  1.7 0.1 broadcast_in_dim.13
  1.8 0.0 copy-start
  1.8 0.6 copy.16
  2.5 0.8 fusion.o_ref
  3.3 0.0 copy-done
  3.3 0.3 copy.17
  3.6 122.7 %shard_map.67 = (f32[512,512]{1,0:T(8,128)S(1)}, f32[8,128]{1,0:T(8,128)S(1)}) custom-call(bf16[12,128,512]{2,1,0:T(8,128)(2,1)} %bitcast.27, bf16[6144,512]{1,0:T(8,128)(2,1)} %bitcast.25, bf16[768,768]{1,0:T(8,128)(2,1)S(1)} %fusion.o_ref, f32[512,512]{1,0:T(8,128)S(1)} %bitcast.23), custom_call_target="tpu_custom_call" | custom-call | tf_op jit(solution)/shard_map/pallas_call | solution.py:225
  126.3 0.7 slice_reduce_fusion
  127.0 1.6 %copy.20 = f32[4,128,512]{2,0,1:T(4,128)} copy(f32[4,128,512]{2,1,0:T(8,128)S(1)} %bitcast.24) | data formatting | bytes 2097152 | tf_op jit(solution)/shard_map/reshape | solution.py:249
  (3 shorter events, 0.0 us)
Async XLA Ops:
  1.8 1.5 %copy-start = (f32[1,128,4,512]{3,2,1,0:T(4,128)S(1)}, f32[1,128,4,512]{3,2,1,0:T(4,128)}, u32[]{:S(2)}) copy-start(f32[1,128,4,512]{3,2,1,0:T(4,128)} %param.7) | copy-start | bytes 3145732

commit v2 on v1

--- a/solution.py
+++ b/solution.py
@@ -41,17 +41,25 @@
 
     depth = width * bond // CHUNKS
 
-    def right_copy(c):
-        rows = pl.ds(c * depth, depth)
+    half = bond // 2
+    each = width // CHUNKS
+
+    def right_view(ref, c, part):
+        if part == 0:
+            return ref.at[pl.ds(c * each, each), pl.ds(0, half), :]
+        return ref.at[pl.ds(c * each, each), pl.ds(half, half), pl.ds(half, half)]
+
+    def right_copy(c, part):
         return pltpu.make_async_remote_copy(
-            src_ref=r_hbm.at[rows], dst_ref=r_ref.at[rows],
-            send_sem=rsend.at[c], recv_sem=rrecv.at[c],
+            src_ref=right_view(r_hbm, c, part), dst_ref=right_view(r_ref, c, part),
+            send_sem=rsend.at[c, part], recv_sem=rrecv.at[c, part],
             device_id={"seg": seg - 1}, device_id_type=MESH,
         )
 
-    def right_local(c):
-        rows = pl.ds(c * depth, depth)
-        return pltpu.make_async_copy(r_hbm.at[rows], r_ref.at[rows], rlocal.at[c])
+    def right_local(c, part):
+        return pltpu.make_async_copy(
+            right_view(r_hbm, c, part), right_view(r_ref, c, part), rlocal.at[c, part]
+        )
 
     def vector_copy(it, way, step, block):
         rows = pl.ds(block * here, here)
@@ -140,14 +148,21 @@
             if it == 0:
                 @pl.when(last)
                 def _():
-                    right_local(c).wait()
+                    for part in range(2):
+                        right_local(c, part).wait()
 
                 @pl.when(jnp.logical_not(last))
                 def _():
-                    right_copy(c).wait_recv()
+                    for part in range(2):
+                        right_copy(c, part).wait_recv()
+
+                @pl.loop(c * each, (c + 1) * each)
+                def _(v):
+                    block = r_ref[v, 0:half, half:bond].astype(jnp.float32)
+                    r_ref[v, half:bond, 0:half] = block.T.astype(jnp.bfloat16)
 
             z = z_ref[:, :, c * depth:(c + 1) * depth].reshape(dp * here, depth)
-            part = jnp.dot(z, r_ref[c * depth:(c + 1) * depth, :], preferred_element_type=jnp.float32)
+            part = jnp.dot(z, r_ref[c * each:(c + 1) * each].reshape(depth, bond), preferred_element_type=jnp.float32)
             if c == 0:
                 y_ref[...] = part
             else:
@@ -157,11 +172,13 @@
     for c in range(CHUNKS):
         @pl.when(seg > 0)
         def _():
-            right_copy(c).start()
+            for part in range(2):
+                right_copy(c, part).start()
 
         @pl.when(last)
         def _():
-            right_local(c).start()
+            for part in range(2):
+                right_local(c, part).start()
 
     apply(0)
     x, y = x_ref[...], y_ref[...]
@@ -204,14 +221,15 @@
     for c in range(CHUNKS):
         @pl.when(seg > 0)
         def _():
-            right_copy(c).wait_send()
+            for part in range(2):
+                right_copy(c, part).wait_send()
 
 
 def local(n, segs, left_env, right_env, site_operator, start_vector):
     _, here, width, bond = left_env.shape
     dp = site_operator.shape[0]
     left = jnp.transpose(left_env[0], (1, 0, 2))
-    right = jnp.transpose(right_env[0], (1, 0, 2)).reshape(width * bond, bond)
+    right = jnp.transpose(right_env[0], (1, 0, 2))
     start = jnp.transpose(start_vector[0], (1, 0, 2)).reshape(dp * here, bond)
     mix = jnp.transpose(site_operator, (1, 0, 3, 2)).reshape(width * dp, dp * width)
     size = width * dp * GROUP
@@ -234,13 +252,13 @@
             pltpu.VMEM((ITERS, dp, n * here, bond), jnp.bfloat16),
             pltpu.VMEM((dp, width, here, bond), jnp.bfloat16),
             pltpu.VMEM((dp, here, width * bond), jnp.bfloat16),
-            pltpu.VMEM((width * bond, bond), jnp.bfloat16),
+            pltpu.VMEM((width, bond, bond), jnp.bfloat16),
             pltpu.VMEM((dp * here, bond), jnp.float32),
             pltpu.VMEM((dp * here, bond), jnp.float32),
             pltpu.VMEM((ITERS, n, 8, 128), jnp.float32),
             dma((ITERS, 2, steps)), dma((ITERS, 2, steps)),
             dma((ITERS, n)), dma((ITERS, n)),
-            dma((CHUNKS,)), dma((CHUNKS,)), dma((CHUNKS,)),
+            dma((CHUNKS, 2)), dma((CHUNKS, 2)), dma((CHUNKS, 2)),
         ],
         compiler_params=pltpu.CompilerParams(
             collective_id=0, has_side_effects=True, vmem_limit_bytes=50 * 2**20

time: 129 us -> 128 us (level)
  the two profiles are of different devices: /device:TPU:5 before, /device:TPU:0 now
where the time goes in v2:
time: 128 us
  Pallas kernels  122 us (95%)
  local copies, waits for them, and re-layouts  4.45 us (3%)
    pallas_call x1, Pallas kernels, local(): pl.pallas_call(functools.partial(kernel, n, segs, dp, width), out_shape=(...  122 us

profile of v2, /device:TPU:0, one launch (start us, length us, event | category | flops | bytes accessed | tf_op | source)
XLA Modules:
  0.0 128.2 jit_solution(5280462861771693123)
XLA Ops:
  0.6 0.8 copy.14
  1.5 0.1 reshape.21
  1.6 0.1 copy.15
  1.7 0.1 broadcast_in_dim.13
  1.8 0.0 copy-start
  1.8 0.6 copy.16
  2.5 0.8 fusion.o_ref
  3.3 0.0 copy-done
  3.3 0.3 copy.17
  3.6 122.3 %shard_map.67 = (f32[512,512]{1,0:T(8,128)S(1)}, f32[8,128]{1,0:T(8,128)S(1)}) custom-call(bf16[12,128,512]{2,1,0:T(8,128)(2,1)} %bitcast.25, bf16[12,512,512]{2,1,0:T(8,128)(2,1)} %bitcast.23, bf16[768,768]{1,0:T(8,128)(2,1)S(1)} %fusion.o_ref, f32[512,512]{1,0:T(8,128)S(1)} %bitcast.21), custom_call_target="tpu_custom_call" | custom-call | tf_op jit(solution)/shard_map/pallas_call | solution.py:243
  125.9 0.7 slice_reduce_fusion
  126.6 1.6 %copy.20 = f32[4,128,512]{2,0,1:T(4,128)} copy(f32[4,128,512]{2,1,0:T(8,128)S(1)} %bitcast.22) | data formatting | bytes 2097152 | tf_op jit(solution)/shard_map/reshape | solution.py:267
  (3 shorter events, 0.0 us)
Async XLA Ops:
  1.8 1.5 %copy-start = (f32[1,128,4,512]{3,2,1,0:T(4,128)S(1)}, f32[1,128,4,512]{3,2,1,0:T(4,128)}, u32[]{:S(2)}) copy-start(f32[1,128,4,512]{3,2,1,0:T(4,128)} %param.7) | copy-start | bytes 3145732

commit v3 on v2

--- a/solution.py
+++ b/solution.py
@@ -36,13 +36,19 @@
             barrier, inc=1, device_id={"seg": lax.rem(seg + k, segs)}, device_id_type=MESH
         )
 
-    xg[0, :, pl.ds(me * here, here), :] = x_ref[...].astype(jnp.bfloat16).reshape(dp, here, bond)
+    half = bond // 2
+
+    def put(it, value):
+        value = value.astype(jnp.bfloat16)
+        for h in range(2):
+            part = value[:, h * half:(h + 1) * half].reshape(dp, here, half)
+            xg[it, h, :, pl.ds(me * here, here), :] = part
+
+    put(0, x_ref[...])
     pl.semaphore_wait(barrier, n + 1)
 
-    depth = width * bond // CHUNKS
-
-    half = bond // 2
     each = width // CHUNKS
+    depth = each * half
 
     def right_view(ref, c, part):
         if part == 0:
@@ -61,11 +67,11 @@
             right_view(r_hbm, c, part), right_view(r_ref, c, part), rlocal.at[c, part]
         )
 
-    def vector_copy(it, way, step, block):
+    def vector_copy(it, h, way, step, block):
         rows = pl.ds(block * here, here)
         return pltpu.make_async_remote_copy(
-            src_ref=xg.at[it, :, rows, :], dst_ref=xg.at[it, :, rows, :],
-            send_sem=gsend.at[it, way, step], recv_sem=grecv.at[it, way, step],
+            src_ref=xg.at[it, h, :, rows, :], dst_ref=xg.at[it, h, :, rows, :],
+            send_sem=gsend.at[it, h, way, step], recv_sem=grecv.at[it, h, way, step],
             device_id={"row": me + (1 if way == 0 else -1)}, device_id_type=MESH,
         )
 
@@ -75,23 +81,23 @@
     def send_down(step):
         return jnp.logical_and(me > 0, me + step <= n - 1)
 
-    def gather_start(it, step):
+    def gather_start(it, h, step):
         @pl.when(send_up(step))
         def _():
-            vector_copy(it, 0, step, me - step).start()
+            vector_copy(it, h, 0, step, me - step).start()
 
         @pl.when(send_down(step))
         def _():
-            vector_copy(it, 1, step, me + step).start()
-
-    def gather_finish(it, step):
+            vector_copy(it, h, 1, step, me + step).start()
+
+    def gather_finish(it, h, step):
         @pl.when(me >= step + 1)
         def _():
-            vector_copy(it, 0, step, me - 1 - step).wait_recv()
+            vector_copy(it, h, 0, step, me - 1 - step).wait_recv()
 
         @pl.when(me + 1 + step <= n - 1)
         def _():
-            vector_copy(it, 1, step, me + 1 + step).wait_recv()
+            vector_copy(it, h, 1, step, me + 1 + step).wait_recv()
 
     def total(parts, it):
         row = lax.broadcasted_iota(jnp.int32, (8, 128), 0)
@@ -122,62 +128,79 @@
             copy.wait_send()
         return [whole[i:i + 1, 0:1] for i in range(len(parts))]
 
-    def apply(it):
-        for step in range(n - 1):
-            if step:
-                gather_start(it, step)
-            gather_finish(it, step)
-
+    def lift(it, h):
         @pl.loop(0, dp * (width // 4))
         def _(i):
             r, m = i // (width // 4), i % (width // 4)
             rows = l_ref[pl.ds(m * 4, 4)].reshape(4 * here, bond)
-            part = jnp.dot(rows, xg[it, r], preferred_element_type=jnp.float32)
-            t_ref[r, pl.ds(m * 4, 4)] = part.astype(jnp.bfloat16).reshape(4, here, bond)
+            part = jnp.dot(rows, xg[it, h, r], preferred_element_type=jnp.float32)
+            t_ref[r, pl.ds(m * 4, 4)] = part.astype(jnp.bfloat16).reshape(4, here, half)
 
         @pl.loop(0, here // GROUP)
         def _(g):
             rows = pl.ds(pl.multiple_of(g * GROUP, GROUP), GROUP)
-            t = t_ref[:, :, rows, :].reshape(dp * width * GROUP, bond)
+            t = t_ref[:, :, rows, :].reshape(dp * width * GROUP, half)
             z = jnp.dot(o_ref[...], t, preferred_element_type=jnp.float32)
-            z = z.astype(jnp.bfloat16).reshape(width, dp, GROUP, bond)
+            z = z.astype(jnp.bfloat16).reshape(width, dp, GROUP, half)
             for v in range(width):
-                z_ref[:, rows, v * bond:(v + 1) * bond] = z[v]
-
+                z_ref[h, :, rows, v * half:(v + 1) * half] = z[v]
+
+    def close(it, h):
         for c in range(CHUNKS):
             if it == 0:
                 @pl.when(last)
                 def _():
-                    for part in range(2):
-                        right_local(c, part).wait()
+                    right_local(c, h).wait()
 
                 @pl.when(jnp.logical_not(last))
                 def _():
-                    for part in range(2):
-                        right_copy(c, part).wait_recv()
-
-                @pl.loop(c * each, (c + 1) * each)
-                def _(v):
-                    block = r_ref[v, 0:half, half:bond].astype(jnp.float32)
-                    r_ref[v, half:bond, 0:half] = block.T.astype(jnp.bfloat16)
-
-            z = z_ref[:, :, c * depth:(c + 1) * depth].reshape(dp * here, depth)
-            part = jnp.dot(z, r_ref[c * each:(c + 1) * each].reshape(depth, bond), preferred_element_type=jnp.float32)
-            if c == 0:
+                    right_copy(c, h).wait_recv()
+
+                if h == 1:
+                    @pl.loop(c * each, (c + 1) * each)
+                    def _(v):
+                        block = r_ref[v, 0:half, half:bond].astype(jnp.float32)
+                        r_ref[v, half:bond, 0:half] = block.T.astype(jnp.bfloat16)
+
+            z = z_ref[h, :, :, c * depth:(c + 1) * depth].reshape(dp * here, depth)
+            r = r_ref[c * each:(c + 1) * each, h * half:(h + 1) * half, :].reshape(depth, bond)
+            part = jnp.dot(z, r, preferred_element_type=jnp.float32)
+            if c == 0 and h == 0:
                 y_ref[...] = part
             else:
                 y_ref[...] += part
 
-    gather_start(0, 0)
-    for c in range(CHUNKS):
-        @pl.when(seg > 0)
-        def _():
-            for part in range(2):
+    def apply(it):
+        for step in range(n - 1):
+            if step:
+                gather_start(it, 0, step)
+            if step == n - 2:
+                gather_start(it, 1, 0)
+            gather_finish(it, 0, step)
+        lift(it, 0)
+        gather_finish(it, 1, 0)
+        if n > 2:
+            gather_start(it, 1, 1)
+        if it > 0:
+            close(it, 0)
+        for step in range(1, n - 1):
+            if step > 1:
+                gather_start(it, 1, step)
+            gather_finish(it, 1, step)
+        lift(it, 1)
+        if it == 0:
+            close(it, 0)
+        close(it, 1)
+
+    gather_start(0, 0, 0)
+    for part in range(2):
+        for c in range(CHUNKS):
+            @pl.when(seg > 0)
+            def _():
                 right_copy(c, part).start()
 
-        @pl.when(last)
-        def _():
-            for part in range(2):
+            @pl.when(last)
+            def _():
                 right_local(c, part).start()
 
     apply(0)
@@ -189,8 +212,8 @@
     beta0 = jnp.sqrt((yy - 2.0 * alpha0 * xy + alpha0 * alpha0 * xx) / entries + 1e-06)
     q = (y_ref[...] * inv - (alpha0 * inv) * x_ref[...]) * (1.0 / beta0)
     q_ref[...] = q
-    xg[1, :, pl.ds(me * here, here), :] = q.astype(jnp.bfloat16).reshape(dp, here, bond)
-    gather_start(1, 0)
+    put(1, q)
+    gather_start(1, 0, 0)
     apply(1)
     x, y, q = x_ref[...] * inv, y_ref[...], q_ref[...]
     yy, yq, yx, qq, qx = total([y * y, y * q, y * x, q * q, q * x], 1)
@@ -209,15 +232,15 @@
         tile = jnp.where(row == i, value, tile)
     scalar_ref[...] = tile
 
-    for it in range(ITERS):
+    for it, h in ((0, 0), (0, 1), (1, 0), (1, 1)):
         for step in range(n - 1):
             @pl.when(send_up(step))
             def _():
-                vector_copy(it, 0, step, me - step).wait_send()
+                vector_copy(it, h, 0, step, me - step).wait_send()
 
             @pl.when(send_down(step))
             def _():
-                vector_copy(it, 1, step, me + step).wait_send()
+                vector_copy(it, h, 1, step, me + step).wait_send()
     for c in range(CHUNKS):
         @pl.when(seg > 0)
         def _():
@@ -249,14 +272,14 @@
         in_specs=[vmem, pl.BlockSpec(memory_space=pl.ANY), vmem, vmem],
         out_specs=(vmem, vmem),
         scratch_shapes=[
-            pltpu.VMEM((ITERS, dp, n * here, bond), jnp.bfloat16),
-            pltpu.VMEM((dp, width, here, bond), jnp.bfloat16),
-            pltpu.VMEM((dp, here, width * bond), jnp.bfloat16),
+            pltpu.VMEM((ITERS, 2, dp, n * here, bond // 2), jnp.bfloat16),
+            pltpu.VMEM((dp, width, here, bond // 2), jnp.bfloat16),
+            pltpu.VMEM((2, dp, here, width * bond // 2), jnp.bfloat16),
             pltpu.VMEM((width, bond, bond), jnp.bfloat16),
             pltpu.VMEM((dp * here, bond), jnp.float32),
             pltpu.VMEM((dp * here, bond), jnp.float32),
             pltpu.VMEM((ITERS, n, 8, 128), jnp.float32),
-            dma((ITERS, 2, steps)), dma((ITERS, 2, steps)),
+            dma((ITERS, 2, 2, steps)), dma((ITERS, 2, 2, steps)),
             dma((ITERS, n)), dma((ITERS, n)),
             dma((CHUNKS, 2)), dma((CHUNKS, 2)), dma((CHUNKS, 2)),
         ],

time: 128 us -> 118 us (0.922)
  the two profiles are of different devices: /device:TPU:0 before, /device:TPU:4 now
where the time goes in v3:
time: 118 us
  Pallas kernels  112 us (95%)
  local copies, waits for them, and re-layouts  4.45 us (4%)
    pallas_call x1, Pallas kernels, local(): pl.pallas_call(functools.partial(kernel, n, segs, dp, width), out_shape=(...  112 us

profile of v3, /device:TPU:4, one launch (start us, length us, event | category | flops | bytes accessed | tf_op | source)
XLA Modules:
  0.0 118.0 jit_solution(410782114485528483)
XLA Ops:
  0.6 0.8 copy.14
  1.5 0.1 reshape.21
  1.6 0.1 copy.15
  1.7 0.1 broadcast_in_dim.13
  1.8 0.0 copy-start
  1.8 0.6 copy.16
  2.5 0.8 fusion.o_ref
  3.3 0.0 copy-done
  3.3 0.3 copy.17
  3.6 112.1 %shard_map.67 = (f32[512,512]{1,0:T(8,128)S(1)}, f32[8,128]{1,0:T(8,128)S(1)}) custom-call(bf16[12,128,512]{2,1,0:T(8,128)(2,1)} %bitcast.25, bf16[12,512,512]{2,1,0:T(8,128)(2,1)} %bitcast.23, bf16[768,768]{1,0:T(8,128)(2,1)S(1)} %fusion.o_ref, f32[512,512]{1,0:T(8,128)S(1)} %bitcast.21), custom_call_target="tpu_custom_call" | custom-call | tf_op jit(solution)/shard_map/pallas_call | solution.py:266
  115.7 0.7 slice_reduce_fusion
  116.4 1.6 %copy.20 = f32[4,128,512]{2,0,1:T(4,128)} copy(f32[4,128,512]{2,1,0:T(8,128)S(1)} %bitcast.22) | data formatting | bytes 2097152 | tf_op jit(solution)/shard_map/reshape | solution.py:290
  (3 shorter events, 0.0 us)
Async XLA Ops:
  1.8 1.5 %copy-start = (f32[1,128,4,512]{3,2,1,0:T(4,128)S(1)}, f32[1,128,4,512]{3,2,1,0:T(4,128)}, u32[]{:S(2)}) copy-start(f32[1,128,4,512]{3,2,1,0:T(4,128)} %param.7) | copy-start | bytes 3145732

commit v4 on v3

--- a/solution.py
+++ b/solution.py
@@ -177,14 +177,18 @@
             if step == n - 2:
                 gather_start(it, 1, 0)
             gather_finish(it, 0, step)
-        lift(it, 0)
         gather_finish(it, 1, 0)
         if n > 2:
             gather_start(it, 1, 1)
+        lift(it, 0)
+        if n > 2:
+            gather_finish(it, 1, 1)
+        if n > 3:
+            gather_start(it, 1, 2)
         if it > 0:
             close(it, 0)
-        for step in range(1, n - 1):
-            if step > 1:
+        for step in range(2, n - 1):
+            if step > 2:
                 gather_start(it, 1, step)
             gather_finish(it, 1, step)
         lift(it, 1)

time: 118 us -> 118 us (level)
  no operation moved by 1% of the time
where the time goes in v4:
time: 118 us
  Pallas kernels  112 us (95%)
  local copies, waits for them, and re-layouts  4.45 us (4%)
    pallas_call x1, Pallas kernels, local(): pl.pallas_call(functools.partial(kernel, n, segs, dp, width), out_shape=(...  112 us

profile of v4, /device:TPU:4, one launch (start us, length us, event | category | flops | bytes accessed | tf_op | source)
XLA Modules:
  0.0 118.0 jit_solution(7228772601507577331)
XLA Ops:
  0.6 0.8 copy.14
  1.5 0.1 reshape.21
  1.6 0.1 copy.15
  1.7 0.1 broadcast_in_dim.13
  1.8 0.0 copy-start
  1.8 0.6 copy.16
  2.5 0.8 fusion.o_ref
  3.3 0.0 copy-done
  3.3 0.3 copy.17
  3.6 112.1 %shard_map.67 = (f32[512,512]{1,0:T(8,128)S(1)}, f32[8,128]{1,0:T(8,128)S(1)}) custom-call(bf16[12,128,512]{2,1,0:T(8,128)(2,1)} %bitcast.25, bf16[12,512,512]{2,1,0:T(8,128)(2,1)} %bitcast.23, bf16[768,768]{1,0:T(8,128)(2,1)S(1)} %fusion.o_ref, f32[512,512]{1,0:T(8,128)S(1)} %bitcast.21), custom_call_target="tpu_custom_call" | custom-call | tf_op jit(solution)/shard_map/pallas_call | solution.py:270
  115.7 0.7 slice_reduce_fusion
  116.4 1.6 %copy.20 = f32[4,128,512]{2,0,1:T(4,128)} copy(f32[4,128,512]{2,1,0:T(8,128)S(1)} %bitcast.22) | data formatting | bytes 2097152 | tf_op jit(solution)/shard_map/reshape | solution.py:294
  (3 shorter events, 0.0 us)
Async XLA Ops:
  1.8 1.5 %copy-start = (f32[1,128,4,512]{3,2,1,0:T(4,128)S(1)}, f32[1,128,4,512]{3,2,1,0:T(4,128)}, u32[]{:S(2)}) copy-start(f32[1,128,4,512]{3,2,1,0:T(4,128)} %param.7) | copy-start | bytes 3145732

commit v5 on v4

--- a/solution.py
+++ b/solution.py
@@ -36,7 +36,7 @@
             barrier, inc=1, device_id={"seg": lax.rem(seg + k, segs)}, device_id_type=MESH
         )
 
-    half = bond // 2
+    half, quarter = bond // 2, bond // 4
 
     def put(it, value):
         value = value.astype(jnp.bfloat16)
@@ -51,9 +51,8 @@
     depth = each * half
 
     def right_view(ref, c, part):
-        if part == 0:
-            return ref.at[pl.ds(c * each, each), pl.ds(0, half), :]
-        return ref.at[pl.ds(c * each, each), pl.ds(half, half), pl.ds(half, half)]
+        rows, columns = pl.ds(part * quarter, quarter), pl.ds(part * quarter, bond - part * quarter)
+        return ref.at[pl.ds(c * each, each), rows, columns]
 
     def right_copy(c, part):
         return pltpu.make_async_remote_copy(
@@ -148,19 +147,25 @@
     def close(it, h):
         for c in range(CHUNKS):
             if it == 0:
+                parts = (2 * h, 2 * h + 1)
+
                 @pl.when(last)
                 def _():
-                    right_local(c, h).wait()
+                    for part in parts:
+                        right_local(c, part).wait()
 
                 @pl.when(jnp.logical_not(last))
                 def _():
-                    right_copy(c, h).wait_recv()
-
-                if h == 1:
-                    @pl.loop(c * each, (c + 1) * each)
-                    def _(v):
-                        block = r_ref[v, 0:half, half:bond].astype(jnp.float32)
-                        r_ref[v, half:bond, 0:half] = block.T.astype(jnp.bfloat16)
+                    for part in parts:
+                        right_copy(c, part).wait_recv()
+
+                @pl.loop(c * each, (c + 1) * each)
+                def _(v):
+                    for part in parts:
+                        if part > 0:
+                            edge = part * quarter
+                            block = r_ref[v, 0:edge, edge:edge + quarter].astype(jnp.float32)
+                            r_ref[v, edge:edge + quarter, 0:edge] = block.T.astype(jnp.bfloat16)
 
             z = z_ref[h, :, :, c * depth:(c + 1) * depth].reshape(dp * here, depth)
             r = r_ref[c * each:(c + 1) * each, h * half:(h + 1) * half, :].reshape(depth, bond)
@@ -197,15 +202,17 @@
         close(it, 1)
 
     gather_start(0, 0, 0)
-    for part in range(2):
+    for h in range(2):
         for c in range(CHUNKS):
             @pl.when(seg > 0)
             def _():
-                right_copy(c, part).start()
+                for part in (2 * h, 2 * h + 1):
+                    right_copy(c, part).start()
 
             @pl.when(last)
             def _():
-                right_local(c, part).start()
+                for part in (2 * h, 2 * h + 1):
+                    right_local(c, part).start()
 
     apply(0)
     x, y = x_ref[...], y_ref[...]
@@ -248,7 +255,7 @@
     for c in range(CHUNKS):
         @pl.when(seg > 0)
         def _():
-            for part in range(2):
+            for part in range(4):
                 right_copy(c, part).wait_send()
 
 
@@ -285,7 +292,7 @@
             pltpu.VMEM((ITERS, n, 8, 128), jnp.float32),
             dma((ITERS, 2, 2, steps)), dma((ITERS, 2, 2, steps)),
             dma((ITERS, n)), dma((ITERS, n)),
-            dma((CHUNKS, 2)), dma((CHUNKS, 2)), dma((CHUNKS, 2)),
+            dma((CHUNKS, 4)), dma((CHUNKS, 4)), dma((CHUNKS, 4)),
         ],
         compiler_params=pltpu.CompilerParams(
             collective_id=0, has_side_effects=True, vmem_limit_bytes=50 * 2**20

time: 118 us -> 119 us (level)
  no operation moved by 1% of the time
where the time goes in v5:
time: 119 us; the launch traced here: 118 us
  Pallas kernels  112 us (94%)
  local copies, waits for them, and re-layouts  4.45 us (4%)
    pallas_call x1, Pallas kernels, local(): pl.pallas_call(functools.partial(kernel, n, segs, dp, width), out_shape=(...  112 us

profile of v5, /device:TPU:4, one launch (start us, length us, event | category | flops | bytes accessed | tf_op | source)
XLA Modules:
  0.0 118.1 jit_solution(6749189001687195081)
XLA Ops:
  0.6 0.8 copy.14
  1.5 0.1 reshape.21
  1.6 0.1 copy.15
  1.7 0.1 broadcast_in_dim.13
  1.8 0.0 copy-start
  1.8 0.6 copy.16
  2.5 0.8 fusion.o_ref
  3.3 0.0 copy-done
  3.3 0.3 copy.17
  3.6 112.1 %shard_map.67 = (f32[512,512]{1,0:T(8,128)S(1)}, f32[8,128]{1,0:T(8,128)S(1)}) custom-call(bf16[12,128,512]{2,1,0:T(8,128)(2,1)} %bitcast.25, bf16[12,512,512]{2,1,0:T(8,128)(2,1)} %bitcast.23, bf16[768,768]{1,0:T(8,128)(2,1)S(1)} %fusion.o_ref, f32[512,512]{1,0:T(8,128)S(1)} %bitcast.21), custom_call_target="tpu_custom_call" | custom-call | tf_op jit(solution)/shard_map/pallas_call | solution.py:277
  115.8 0.7 slice_reduce_fusion
  116.4 1.6 %copy.20 = f32[4,128,512]{2,0,1:T(4,128)} copy(f32[4,128,512]{2,1,0:T(8,128)S(1)} %bitcast.22) | data formatting | bytes 2097152 | tf_op jit(solution)/shard_map/reshape | solution.py:301
  (3 shorter events, 0.0 us)
Async XLA Ops:
  1.8 1.5 %copy-start = (f32[1,128,4,512]{3,2,1,0:T(4,128)S(1)}, f32[1,128,4,512]{3,2,1,0:T(4,128)}, u32[]{:S(2)}) copy-start(f32[1,128,4,512]{3,2,1,0:T(4,128)} %param.7) | copy-start | bytes 3145732
